TPU v7x, 128 devices: a whole 4x4x4 slice. The times are simulated.
128 devices in a mesh: expert: 32 (over x, z, core), shard: 4 (over y).
Axes of the slice: x: 4, y: 4, z: 4, core: 2. Of those that a mesh axis runs over, the one named last changes fastest.
Arguments:
- tokens: bfloat16 [16384, 768], P('expert'), may hold values from -6 to 6
- qkv_weight: bfloat16 [3, 768, 768], P(None, None, 'shard'), may hold values from -0.21875 to 0.21875
- out_proj: bfloat16 [768, 768], P('shard'), may hold values from -0.875 to 0.875
- rel_bias: float32 [12, 32], P('shard'), may hold values from -6 to 6
- gains: float32 [2, 768], replicated, may hold values from 0.5 to 1.5
- router: bfloat16 [768, 32], replicated, may hold values from -0.109375 to 0.109375
- w_in: bfloat16 [32, 768, 3072], P('expert', None, 'shard'), may hold values from -0.21875 to 0.21875
- w_out: bfloat16 [32, 3072, 768], P('expert', 'shard'), may hold values from -7 to 7
- route: int32 [16384], P('expert'), may hold values from 0 to 31, as said below
- slot: int32 [16384], P('expert'), may hold values from 0 to 23, as said below
- buckets: int32 [1023], replicated, may hold values from 0 to 31, as said below
- cotangent: bfloat16 [16384, 768], P('expert'), may hold values from -6 to 6
Outputs:
- result: bfloat16 [16384, 768], P('expert')
- grad_tokens: bfloat16 [16384, 768], P('expert')
- grad_qkv: float32 [3, 768, 768], P(None, None, 'shard')
- grad_out_proj: float32 [768, 768], P('shard')
- grad_bias: float32 [12, 32], P('shard')
- grad_gains: float32 [2, 768], replicated
- grad_router: float32 [768, 32], replicated
- grad_w_in: float32 [32, 768, 3072], P('expert', None, 'shard')
- grad_w_out: float32 [32, 3072, 768], P('expert', 'shard')
Inputs may be any that keep to these rules, and one draw needn't show every extreme that they name: Within each aligned block of 512 rows (one sequence) no two rows share both route and slot, and in every block some expert has all 24 slots taken. `slot`: paired with route as stated there. Entry j - i + 511 is the bucket of offset j - i: 0 for offset 0, buckets 0 to 15 for offsets of at most 0 and the rest for positive ones, never falling with the size of the offset within one sign.
All inputs are finite; a program needn't handle non-finite values.
Results may differ from a plain program's by a relative error of at most 0.03.
Values may be sent and summed in bfloat16 or wider, within the bound.
No kernel may reach another device: no remote copies, remote signals or barrier semaphores. Data moves between devices by JAX's collectives and lax.ppermute only.
A program may use at most 128 MiB of HBM per device.

v0:
```python
import jax
import jax.numpy as jnp
from jax import lax
from jax.sharding import PartitionSpec as P

HEAD_DIM = 64
BUCKETS = 32


EPS = 1e-06


def normalize(values, gain_vec):
    return values * lax.rsqrt(jnp.mean(values * values, axis=-1, keepdims=True) + EPS) * gain_vec


def send_rows(outgoing):
    return lax.all_to_all(outgoing, "expert", split_axis=0, concat_axis=0, tiled=True)


def return_home(partial_value, route, slot):
    returned = lax.all_to_all(
        partial_value.astype(jnp.bfloat16), "expert", split_axis=0, concat_axis=0, tiled=True
    ).astype(partial_value.dtype)
    by_expert = returned.reshape(-1, returned.shape[2], returned.shape[3])
    summed = lax.psum(by_expert[route, slot].astype(jnp.bfloat16), "shard")
    return lax.optimization_barrier(summed).astype(jnp.float32)


def local(
    tokens,
    qkv_weight,
    out_proj,
    rel_bias,
    gains,
    router,
    w_in,
    w_out,
    route,
    slot,
    buckets,
    cotangent,
):
    highest = lax.Precision.HIGHEST
    length, feature_width = tokens.shape
    local_width = out_proj.shape[0]
    heads_local = local_width // HEAD_DIM
    experts = router.shape[1]
    owners = lax.axis_size("expert")
    capacity = max(2, 3 * length // (2 * experts))
    row_block = min(512, length)
    num_blocks = length // row_block
    score_scale = HEAD_DIM ** (-0.5)
    bias_span = length + row_block - 1
    x_float = tokens.astype(jnp.float32)
    normed, norm_back = jax.vjp(normalize, x_float, gains[0])
    normed_b = normed.astype(jnp.bfloat16)
    projected = jnp.einsum(
        "td,cde->cte", normed_b, qkv_weight, preferred_element_type=jnp.float32
    ).astype(jnp.bfloat16)
    qry_rows = projected[0].reshape(length, heads_local, HEAD_DIM)
    key_rows = projected[1].reshape(length, heads_local, HEAD_DIM)
    val_rows = projected[2].reshape(length, heads_local, HEAD_DIM)
    bucket_hot = (buckets[None, :] == jnp.arange(BUCKETS, dtype=jnp.int32)[:, None]).astype(
        jnp.float32
    )
    offset_bias = jnp.dot(rel_bias, bucket_hot, precision=highest)

    def bias_block():
        padded = jnp.pad(offset_bias, ((0, 0), (0, 1)))
        tiled = jnp.tile(padded, (1, row_block))
        flat = tiled[:, row_block - 1 : row_block - 1 + row_block * bias_span]
        return flat.reshape(heads_local, row_block, bias_span)[:, :, :length]

    def scores_of(q_blk):
        scores = (
            jnp.einsum("qhd,khd->hqk", q_blk, key_rows, preferred_element_type=jnp.float32)
            * score_scale
        )
        return scores + bias_block()

    starts = jnp.arange(num_blocks, dtype=jnp.int32) * row_block
    q_blocks = qry_rows.reshape(num_blocks, row_block, heads_local, HEAD_DIM)

    def forward_block(operands):
        row_start, q_blk = operands
        scores = scores_of(q_blk)
        row_max = jnp.max(scores, axis=-1, keepdims=True)
        expd = jnp.exp(scores - row_max)
        row_total = jnp.sum(expd, axis=-1, keepdims=True)
        weights = (expd / row_total).astype(jnp.bfloat16)
        head_mix = jnp.einsum("hqk,khd->qhd", weights, val_rows, preferred_element_type=jnp.float32)
        log_total = row_max[..., 0] + jnp.log(row_total[..., 0])
        return (head_mix.astype(jnp.bfloat16), log_total)

    head_blocks, log_totals = lax.map(forward_block, (starts, q_blocks))
    heads_out = head_blocks.reshape(length, local_width)
    attention = lax.psum(
        jnp.dot(heads_out, out_proj, preferred_element_type=jnp.float32).astype(jnp.bfloat16),
        "shard",
    ).astype(jnp.float32)
    hidden = x_float + attention
    mixed, mix_back = jax.vjp(normalize, hidden, gains[1])
    mixed_b = mixed.astype(jnp.bfloat16)
    logits = jnp.dot(mixed_b, router, preferred_element_type=jnp.float32)
    router_probs = jax.nn.softmax(logits, axis=-1)
    chosen = (route[:, None] == jnp.arange(experts, dtype=jnp.int32)[None, :]).astype(jnp.float32)
    gate_prob = jnp.sum(router_probs * chosen, axis=1)
    empty_rows = jnp.zeros((experts, capacity, feature_width), jnp.bfloat16)
    outgoing = (
        empty_rows.at[route, slot]
        .set(mixed_b)
        .reshape(owners, experts // owners, capacity, feature_width)
    )
    arrived = send_rows(outgoing)
    pre_act = jnp.einsum("gecd,edf->gecf", arrived, w_in, preferred_element_type=jnp.float32)
    activated, gelu_back = jax.vjp(jax.nn.gelu, pre_act)
    act_b = activated.astype(jnp.bfloat16)
    partial_value = jnp.einsum("gecf,efd->gecd", act_b, w_out, preferred_element_type=jnp.float32)
    expert_out = return_home(partial_value, route, slot)
    result = hidden + gate_prob[:, None] * expert_out
    grad_y = cotangent.astype(jnp.float32)
    grad_gate = jnp.sum(grad_y * expert_out, axis=1)
    grad_expert = (gate_prob[:, None] * grad_y).astype(jnp.bfloat16)
    grad_logits = router_probs * (chosen - gate_prob[:, None]) * grad_gate[:, None]
    grad_router = jnp.einsum(
        "td,te->de", mixed_b.astype(jnp.float32), grad_logits, precision=highest
    )
    grad_mixed = jnp.einsum("te,de->td", grad_logits, router.astype(jnp.float32), precision=highest)
    back_out = (
        empty_rows.at[route, slot]
        .set(grad_expert)
        .reshape(owners, experts // owners, capacity, feature_width)
    )
    back_arrived = send_rows(back_out)
    grad_act = jnp.einsum("gecd,efd->gecf", back_arrived, w_out, preferred_element_type=jnp.float32)
    grad_pre = gelu_back(grad_act)[0].astype(jnp.bfloat16)
    grad_w_out = jnp.einsum(
        "gecf,gecd->efd", act_b, back_arrived, preferred_element_type=jnp.float32
    )
    grad_w_in = jnp.einsum("gecd,gecf->edf", arrived, grad_pre, preferred_element_type=jnp.float32)
    grad_part = jnp.einsum("gecf,edf->gecd", grad_pre, w_in, preferred_element_type=jnp.float32)
    grad_rows = return_home(grad_part, route, slot)
    grad_hidden_norm, grad_gain_two = mix_back(grad_mixed + grad_rows)
    grad_hidden = grad_y + grad_hidden_norm
    grad_attn_b = grad_hidden.astype(jnp.bfloat16)
    grad_out_proj = jnp.einsum(
        "tf,td->fd", heads_out, grad_attn_b, preferred_element_type=jnp.float32
    )
    grad_heads = jnp.einsum(
        "td,fd->tf", grad_attn_b, out_proj, preferred_element_type=jnp.float32
    ).astype(jnp.bfloat16)
    grad_head_blocks = grad_heads.reshape(num_blocks, row_block, heads_local, HEAD_DIM)
    offset_count = 2 * length - 1
    skew_width = length + row_block

    def diagonal_sums(grad_scores_f):
        flipped = jnp.flip(grad_scores_f, axis=2)
        padded = jnp.pad(flipped, ((0, 0), (0, 0), (0, row_block)))
        flat = padded.reshape(heads_local, row_block * skew_width)[
            :, : row_block * (skew_width - 1)
        ]
        skewed = flat.reshape(heads_local, row_block, skew_width - 1)
        return jnp.flip(jnp.sum(skewed, axis=1), axis=1)

    def backward_block(totals, operands):
        grad_keys, grad_vals, grad_offsets = totals
        row_start, q_blk, do_blk, lse_blk = operands
        scores = scores_of(q_blk)
        weights = jnp.exp(scores - lse_blk[..., None])
        weights_b = weights.astype(jnp.bfloat16)
        grad_weights = jnp.einsum(
            "qhd,khd->hqk", do_blk, val_rows, preferred_element_type=jnp.float32
        )
        row_delta = jnp.sum(weights * grad_weights, axis=-1, keepdims=True)
        grad_scores = (weights * (grad_weights - row_delta)).astype(jnp.bfloat16)
        grad_q = (
            jnp.einsum("hqk,khd->qhd", grad_scores, key_rows, preferred_element_type=jnp.float32)
            * score_scale
        )
        grad_keys = (
            grad_keys
            + jnp.einsum("hqk,qhd->khd", grad_scores, q_blk, preferred_element_type=jnp.float32)
            * score_scale
        )
        grad_vals = grad_vals + jnp.einsum(
            "hqk,qhd->khd", weights_b, do_blk, preferred_element_type=jnp.float32
        )
        run_sums = diagonal_sums(grad_scores.astype(jnp.float32))
        current = grad_offsets
        grad_offsets = current + run_sums
        return ((grad_keys, grad_vals, grad_offsets), grad_q)

    zero_rows = jnp.zeros((length, heads_local, HEAD_DIM), jnp.float32)
    zero_offsets = jnp.zeros((heads_local, offset_count), jnp.float32)
    (grad_keys, grad_vals, grad_offsets), grad_queries = lax.scan(
        backward_block,
        (zero_rows, zero_rows, zero_offsets),
        (starts, q_blocks, grad_head_blocks, log_totals),
    )
    grad_proj = jnp.stack(
        [
            grad_queries.reshape(length, local_width),
            grad_keys.reshape(length, local_width),
            grad_vals.reshape(length, local_width),
        ]
    ).astype(jnp.bfloat16)
    grad_qkv = jnp.einsum("td,cte->cde", normed_b, grad_proj, preferred_element_type=jnp.float32)
    grad_normed = lax.psum(
        jnp.einsum("cte,cde->td", grad_proj, qkv_weight, preferred_element_type=jnp.float32).astype(
            jnp.bfloat16
        ),
        "shard",
    ).astype(jnp.float32)
    grad_x_norm, grad_gain_one = norm_back(grad_normed)
    grad_tokens = (grad_hidden + grad_x_norm).astype(jnp.bfloat16)
    grad_bias = jnp.einsum("ho,bo->hb", grad_offsets, bucket_hot, precision=highest)
    grad_gains = jnp.stack([grad_gain_one, grad_gain_two])
    grad_qkv, grad_out_proj, grad_bias, grad_gains, grad_router = (
        lax.psum(grad_qkv.astype(jnp.bfloat16), "expert").astype(jnp.float32),
        lax.psum(grad_out_proj.astype(jnp.bfloat16), "expert").astype(jnp.float32),
        lax.psum(grad_bias.astype(jnp.bfloat16), "expert").astype(jnp.float32),
        lax.psum(grad_gains.astype(jnp.bfloat16), "expert").astype(jnp.float32),
        lax.psum(grad_router.astype(jnp.bfloat16), "expert").astype(jnp.float32),
    )
    return (
        result.astype(jnp.bfloat16),
        grad_tokens,
        grad_qkv,
        grad_out_proj,
        grad_bias,
        grad_gains,
        grad_router,
        grad_w_in,
        grad_w_out,
    )


def solution(mesh):
    in_specs = (
        P("expert", None),
        P(None, None, "shard"),
        P("shard", None),
        P("shard", None),
        P(),
        P(),
        P("expert", None, "shard"),
        P("expert", "shard", None),
        P("expert"),
        P("expert"),
        P(),
        P("expert", None),
    )
    out_specs = (
        P("expert", None),
        P("expert", None),
        P(None, None, "shard"),
        P("shard", None),
        P("shard", None),
        P(),
        P(),
        P("expert", None, "shard"),
        P("expert", "shard", None),
    )
    return jax.shard_map(local, mesh=mesh, in_specs=in_specs, out_specs=out_specs, check_vma=False)
```

profile of v0, /device:TPU:0, one launch (start us, length us, event | category | flops | bytes accessed | tf_op | source)
XLA Modules:
  0.0 689.7 jit_solution(14410891289692366737)
XLA Ops:
  10.1 2.1 fusion.56
  13.3 3.4 broadcast_bitcast_fusion
  16.8 7.1 %copy.56 = f32[1,3,512,1024]{3,1,2,0:T(4,128)S(1)} copy(f32[1,3,512,1024]{3,2,1,0:T(8,128)} %broadcast_bitcast_fusion) | data formatting | bytes 12582912
  23.9 6.4 slice.50
  30.3 13.2 %reshape.149 = f32[3,512,1023]{2,1,0:T(8,128)} reshape(f32[3,523776]{1,0:T(4,128)} %slice.50) | data formatting | bytes 12570624 | tf_op jit(solution)/shard_map/while/body/eval_jaxpr/reshape | solution.py:73
  43.5 3.8 slice.51
  47.3 3.6 copy.54
  50.9 2.5 fusion.84
  57.8 47.0 %all-reduce.10.cloned.1.call-done = bf16[512,768]{1,0:T(8,128)(2,1)} async-done(((bf16[512,768]{1,0:T(8,128)(2,1)}), bf16[512,768]{1,0:T(8,128)(2,1)}) %all-reduce.10.cloned.1.call-update) | async-done | bytes 786448 | tf_op jit(solution)/shard_map/psum | solution.py:98
  104.8 1.5 multiply_reduce_fusion.3
  107.9 67.8 %scatter_fusion = bf16[32,24,768]{2,1,0:T(8,128)(2,1)} fusion(bf16[32,24,768]{2,1,0:T(8,128)(2,1)} %broadcast_in_dim.24.clone, s32[512]{0:T(512)S(1)} %bitcast.182, bf16[512,768]{1,0:T(8,128)(2,1)S(1)} %multiply_convert_fusion.1), kind=kCustom, calls=%fused_computation.2 | custom fusion | bytes 2363392 | tf_op jit(solution)/shard_map/scatter | solution.py:112
  175.8 7.4 %all-to-all-start = ((bf16[32,1,24,768]{3,2,1,0:T(8,128)(2,1)}), bf16[32,1,24,768]{3,2,1,0:T(8,128)(2,1)}, u32[]{:S(2)}, u32[]{:S(2)}) async-start(bf16[32,1,24,768]{3,2,1,0:T(8,128)(2,1)} %bitcast.13), calls=%async_computation | async-start | bytes 2359296 | tf_op jit(solution)/shard_map/all_to_all | solution.py:18
  188.0 67.8 %scatter_fusion.1 = bf16[32,24,768]{2,1,0:T(8,128)(2,1)} fusion(bf16[32,24,768]{2,1,0:T(8,128)(2,1)} %broadcast_in_dim.24.clone.1, s32[512]{0:T(512)S(1)} %bitcast.183, bf16[512,768]{1,0:T(8,128)(2,1)S(1)} %fusion.20), kind=kCustom, calls=%fused_computation.3 | custom fusion | bytes 2363392 | tf_op jit(solution)/shard_map/scatter | solution.py:132
  255.8 7.3 %all-to-all-start.2 = ((bf16[32,1,24,768]{3,2,1,0:T(8,128)(2,1)}), bf16[32,1,24,768]{3,2,1,0:T(8,128)(2,1)S(1)}, u32[]{:S(2)}, u32[]{:S(2)}) async-start(bf16[32,1,24,768]{3,2,1,0:T(8,128)(2,1)} %bitcast.33), calls=%async_computation.2 | async-start | bytes 2359296 | tf_op jit(solution)/shard_map/all_to_all | solution.py:18
  263.1 2.7 fusion.40
  267.2 2.7 fusion.29
  270.0 11.5 %all-to-all-done.2 = bf16[32,1,24,768]{3,2,1,0:T(8,128)(2,1)S(1)} async-done(((bf16[32,1,24,768]{3,2,1,0:T(8,128)(2,1)}), bf16[32,1,24,768]{3,2,1,0:T(8,128)(2,1)S(1)}, u32[]{:S(2)}, u32[]{:S(2)}) %all-to-all-start.2) | async-done | bytes 1179680 | tf_op jit(solution)/shard_map/all_to_all | solution.py:18
  282.5 3.9 all-to-all-start.1
  286.4 4.3 fusion.31
  291.8 2.2 fusion.30
  294.0 10.7 %all-to-all-done.1 = bf16[32,1,24,768]{3,2,1,0:T(8,128)(2,1)S(1)} async-done(((bf16[32,1,24,768]{3,2,1,0:T(8,128)(2,1)}), bf16[32,1,24,768]{3,2,1,0:T(8,128)(2,1)S(1)}, u32[]{:S(2)}, u32[]{:S(2)}) %all-to-all-start.1) | async-done | bytes 1179680 | tf_op jit(solution)/shard_map/all_to_all | solution.py:22
  304.8 3.9 all-to-all-start.3
  308.8 7.2 %gather_fusion = bf16[512,768]{1,0:T(8,128)(2,1)} fusion(bf16[32,24,768]{2,1,0:T(8,128)(2,1)S(1)} %bitcast.184, s32[512]{0:T(512)S(1)} %bitcast.180), kind=kCustom, calls=%fused_computation | custom fusion | bytes 1576960 | tf_op jit(solution)/shard_map/gather | solution.py:26
  316.0 11.1 %all-to-all-done.3 = bf16[32,1,24,768]{3,2,1,0:T(8,128)(2,1)S(1)} async-done(((bf16[32,1,24,768]{3,2,1,0:T(8,128)(2,1)}), bf16[32,1,24,768]{3,2,1,0:T(8,128)(2,1)S(1)}, u32[]{:S(2)}, u32[]{:S(2)}) %all-to-all-start.3) | async-done | bytes 1179680 | tf_op jit(solution)/shard_map/all_to_all | solution.py:22
  327.1 7.2 %gather_fusion.1 = bf16[512,768]{1,0:T(8,128)(2,1)} fusion(bf16[32,24,768]{2,1,0:T(8,128)(2,1)S(1)} %bitcast.185, s32[512]{0:T(512)S(1)} %bitcast.181), kind=kCustom, calls=%fused_computation.1 | custom fusion | bytes 1576960 | tf_op jit(solution)/shard_map/gather | solution.py:26
  335.0 47.7 %all-reduce.16.cloned.1.call-done = (bf16[512,768]{1,0:T(8,128)(2,1)}, bf16[512,768]{1,0:T(8,128)(2,1)}) async-done(((bf16[512,768]{1,0:T(8,128)(2,1)}, bf16[512,768]{1,0:T(8,128)(2,1)}), (bf16[512,768]{1,0:T(8,128)(2,1)}, bf16[512,768]{1,0:T(8,128)(2,1)})) %all-reduce.16.cloned.1.call-update) | async-done | bytes 1572880 | tf_op jit(solution)/shard_map/psum | solution.py:26
  382.7 1.5 fusion.19
  384.3 1.9 multiply_reduce_fusion.1
  386.3 1.6 convert_add_fusion.1
  395.2 1.7 fusion.32
  397.2 4.5 convolution_bitcast_fusion
  401.7 1.7 bitcast_convert_fusion
  403.5 3.8 convolution_bitcast_fusion.1
  407.3 15.7 %rev.10 = f32[3,512,512]{1,2,0:T(8,128)} reverse(bf16[3,512,512]{1,2,0:T(8,128)(2,1)S(1)} %multiply_convert_fusion), dimensions={2} | reverse | bytes 4718592 | tf_op jit(solution)/shard_map/while/body/eval_jaxpr/jit(_flip)/rev | solution.py:158
  423.0 3.6 copy.55
  426.6 5.4 pad_bitcast_fusion
  432.0 7.1 %copy.57 = f32[1,3,512,1024]{3,1,2,0:T(4,128)S(1)} copy(f32[1,3,512,1024]{3,2,1,0:T(8,128)} %pad_bitcast_fusion) | data formatting | bytes 12582912
  439.1 4.3 slice.52
  443.4 13.3 %reshape.164 = f32[3,512,1023]{2,1,0:T(8,128)} reshape(f32[3,523776]{1,0:T(4,128)} %slice.52) | data formatting | bytes 12570624 | tf_op jit(solution)/shard_map/while/body/eval_jaxpr/reshape | solution.py:163
  456.7 3.3 reduce_sum.136
  461.5 40.8 %all-reduce.14.cloned.1.call-done = (bf16[3,768,192]{1,2,0:T(8,128)(2,1)}, bf16[192,768]{1,0:T(8,128)(2,1)}) async-done(((bf16[3,768,192]{1,2,0:T(8,128)(2,1)}, bf16[192,768]{1,0:T(8,128)(2,1)}), (bf16[3,768,192]{1,2,0:T(8,128)(2,1)}, bf16[192,768]{1,0:T(8,128)(2,1)})) %all-reduce.14.cloned.1.call-update) | async-done | bytes 1179664 | tf_op jit(solution)/shard_map/psum | solution.py:220
  502.3 1.9 convert_element_type.196
  504.2 2.5 convert_element_type.194
  506.7 42.4 %all-reduce.12.cloned.1.call-done = bf16[512,768]{1,0:T(8,128)(2,1)} async-done(((bf16[512,768]{1,0:T(8,128)(2,1)}), bf16[512,768]{1,0:T(8,128)(2,1)}) %all-reduce.12.cloned.1.call-update) | async-done | bytes 786448 | tf_op jit(solution)/shard_map/psum | solution.py:209
  549.1 1.9 fusion.18
  551.1 126.6 %all-reduce.2 = (bf16[3,32]{1,0:T(4,128)(2,1)S(1)}, bf16[2,768]{1,0:T(2,128)(2,1)S(1)}, bf16[768,32]{0,1:T(8,128)(2,1)}) all-reduce(bf16[3,32]{1,0:T(4,128)(2,1)S(1)} %convolution_convert_fusion.7, bf16[2,768]{1,0:T(2,128)(2,1)S(1)} %pad_maximum_fusion.3, ...), channel_id=1, replica_groups=mesh['expert'=32,'shard'=4] {'expert'}, use_global_device_ids=true, to_apply=%region_20.21 | all-reduce | flops 26208 | bytes 104832 | tf_op jit(solution)/shard_map/psum | solution.py:222
  678.9 1.5 convert_element_type.202
  680.5 2.5 fusion.22
  (194 shorter events, 28.7 us)
Async XLA Ops:
  7.2 260.0 %copy-start = (bf16[1,768,768]{2,1,0:T(8,128)(2,1)S(1)}, bf16[1,768,768]{2,1,0:T(8,128)(2,1)}, u32[]{:S(2)}) copy-start(bf16[1,768,768]{2,1,0:T(8,128)(2,1)} %param.19) | copy-start | bytes 3538948
  7.2 97.6 %all-reduce.10.cloned.1.call-start = ((), (), s32[]{:S(2)}) async-start(), calls=%async_computation.4 | async-start | bytes 1572864 | tf_op jit(solution)/shard_map/psum | solution.py:98
  9.3 3.0 copy-start.48
  10.1 2.2 copy-start.39
  10.1 96.3 %copy-start.37 = (f32[768]{0:T(1024)}, f32[768]{0:T(1024)S(1)}, u32[]{:S(2)}) copy-start(f32[768]{0:T(1024)S(1)} %get-tuple-element.56) | copy-start | bytes 9220
  13.1 37.8 %copy-start.15 = (bf16[1,512,192]{1,2,0:T(8,128)(2,1)}, bf16[1,512,192]{1,2,0:T(8,128)(2,1)S(1)}, u32[]{:S(2)}) copy-start(bf16[1,512,192]{1,2,0:T(8,128)(2,1)S(1)} %get-tuple-element.78) | copy-start | bytes 589828
  47.3 3.6 copy-start.17
  55.8 2.0 copy-start.53
  55.8 49.0 %copy-start.4 = (bf16[512,768]{1,0:T(8,128)(2,1)S(1)}, bf16[512,768]{1,0:T(8,128)(2,1)}, u32[]{:S(2)}) copy-start(bf16[512,768]{1,0:T(8,128)(2,1)} %param.12) | copy-start | bytes 2359300
  106.7 76.5 %copy-start.8 = (bf16[512,768]{1,0:T(8,128)(2,1)}, bf16[512,768]{1,0:T(8,128)(2,1)S(1)}, u32[]{:S(2)}) copy-start(bf16[512,768]{1,0:T(8,128)(2,1)S(1)} %multiply_convert_fusion.1) | copy-start | bytes 2359300
  175.8 10.5 %copy-start.10 = (bf16[512,768]{1,0:T(8,128)(2,1)S(1)}, bf16[512,768]{1,0:T(8,128)(2,1)}, u32[]{:S(2)}) copy-start(bf16[512,768]{1,0:T(8,128)(2,1)} %param.23) | copy-start | bytes 2359300
  175.8 80.0 %all-to-all-start = ((bf16[32,1,24,768]{3,2,1,0:T(8,128)(2,1)}), bf16[32,1,24,768]{3,2,1,0:T(8,128)(2,1)}, u32[]{:S(2)}, u32[]{:S(2)}) async-start(bf16[32,1,24,768]{3,2,1,0:T(8,128)(2,1)} %bitcast.13), calls=%async_computation | async-start | bytes 2359296 | tf_op jit(solution)/shard_map/all_to_all | solution.py:18
  255.8 25.7 %all-to-all-start.2 = ((bf16[32,1,24,768]{3,2,1,0:T(8,128)(2,1)}), bf16[32,1,24,768]{3,2,1,0:T(8,128)(2,1)S(1)}, u32[]{:S(2)}, u32[]{:S(2)}) async-start(bf16[32,1,24,768]{3,2,1,0:T(8,128)(2,1)} %bitcast.33), calls=%async_computation.2 | async-start | bytes 2359296 | tf_op jit(solution)/shard_map/all_to_all | solution.py:18
  282.5 22.3 %all-to-all-start.1 = ((bf16[32,1,24,768]{3,2,1,0:T(8,128)(2,1)}), bf16[32,1,24,768]{3,2,1,0:T(8,128)(2,1)S(1)}, u32[]{:S(2)}, u32[]{:S(2)}) async-start(bf16[32,1,24,768]{3,2,1,0:T(8,128)(2,1)} %fusion.29), calls=%async_computation.1 | async-start | bytes 2359296 | tf_op jit(solution)/shard_map/all_to_all | solution.py:22
  286.4 5.4 copy-start.64
  304.8 22.3 %all-to-all-start.3 = ((bf16[32,1,24,768]{3,2,1,0:T(8,128)(2,1)}), bf16[32,1,24,768]{3,2,1,0:T(8,128)(2,1)S(1)}, u32[]{:S(2)}, u32[]{:S(2)}) async-start(bf16[32,1,24,768]{3,2,1,0:T(8,128)(2,1)} %fusion.30), calls=%async_computation.3 | async-start | bytes 2359296 | tf_op jit(solution)/shard_map/all_to_all | solution.py:22
  308.7 74.0 %all-reduce.16.cloned.1.call-start = ((), (), s32[]{:S(2)}) async-start(), calls=%async_computation.7 | async-start | bytes 3145728 | tf_op jit(solution)/shard_map/psum | solution.py:26
  334.3 48.4 %copy-start.11 = (bf16[512,768]{1,0:T(8,128)(2,1)S(1)}, bf16[512,768]{1,0:T(8,128)(2,1)}, u32[]{:S(2)}) copy-start(bf16[512,768]{1,0:T(8,128)(2,1)} %param.23) | copy-start | bytes 2359300
  334.3 49.9 %copy-start.13 = (bf16[512,768]{1,0:T(8,128)(2,1)S(1)}, bf16[512,768]{1,0:T(8,128)(2,1)}, u32[]{:S(2)}) copy-start(bf16[512,768]{1,0:T(8,128)(2,1)} %all-reduce.10.cloned.1.call-done) | copy-start | bytes 2359300
  334.3 49.9 %copy-start.24 = (f32[512,32]{0,1:T(8,128)S(1)}, f32[512,32]{0,1:T(8,128)}, u32[]{:S(2)}) copy-start(f32[512,32]{0,1:T(8,128)} %copy-done.23) | copy-start | bytes 196612
  334.3 49.9 %copy-start.36 = (bf16[768,32]{0,1:T(8,128)(2,1)S(1)}, bf16[768,32]{0,1:T(8,128)(2,1)}, u32[]{:S(2)}) copy-start(bf16[768,32]{0,1:T(8,128)(2,1)} %param.17) | copy-start | bytes 147460
  334.3 49.9 %copy-start.38 = (f32[768]{0:T(1024)S(1)}, f32[768]{0:T(1024)}, u32[]{:S(2)}) copy-start(f32[768]{0:T(1024)} %copy-done.37) | copy-start | bytes 9220
  334.3 49.9 %copy-start.42 = (f32[512]{0:T(512)S(1)}, f32[512]{0:T(512)}, u32[]{:S(2)}) copy-start(f32[512]{0:T(512)} %copy-done.41) | copy-start | bytes 6148
  334.3 49.9 %copy-start.46 = (f32[512]{0:T(512)S(1)}, f32[512]{0:T(512)}, u32[]{:S(2)}) copy-start(f32[512]{0:T(512)} %copy-done.45) | copy-start | bytes 6148
  334.3 49.9 %copy-start.51 = (f32[512]{0:T(512)S(1)}, f32[512]{0:T(512)}, u32[]{:S(2)}) copy-start(f32[512]{0:T(512)} %copy-done.50) | copy-start | bytes 6148
  334.4 49.9 %copy-start.54 = (s32[512]{0:T(512)S(1)}, s32[512]{0:T(512)}, u32[]{:S(2)}) copy-start(s32[512]{0:T(512)} %param.20) | copy-start | bytes 6148
  334.4 49.9 %copy-start.61 = (f32[512]{0:T(512)S(1)}, f32[512]{0:T(512)}, u32[]{:S(2)}) copy-start(f32[512]{0:T(512)} %copy-done.60) | copy-start | bytes 6148
  334.4 167.9 %all-reduce.14.cloned.1.call-start = ((), (), s32[]{:S(2)}) async-start(), calls=%async_computation.6 | async-start | bytes 2359296 | tf_op jit(solution)/shard_map/psum | solution.py:220
  388.0 2.6 copy-start.3
  391.5 3.0 copy-start.30
  393.2 2.0 copy-start.40
  393.2 2.0 copy-start.49
  396.9 4.8 copy-start.31
  396.9 4.8 copy-start.33
  396.9 4.8 copy-start.35
  396.9 152.2 %all-reduce.12.cloned.1.call-start = ((), (), s32[]{:S(2)}) async-start(), calls=%async_computation.5 | async-start | bytes 1572864 | tf_op jit(solution)/shard_map/psum | solution.py:209
  397.2 4.5 copy-start.65
  407.3 15.7 %copy-start.63 = (bf16[768]{0:T(1024)(128)(2,1)S(1)}, bf16[768]{0:T(1024)(128)(2,1)}, u32[]{:S(2)}) copy-start(bf16[768]{0:T(1024)(128)(2,1)} %get-tuple-element.52) | copy-start | bytes 4612
  456.7 4.0 copy-start.68
  456.7 4.2 copy-start.9
  456.7 4.2 copy-start.25
  456.7 4.3 copy-start.47
  456.7 4.3 copy-start.52
  456.7 4.3 copy-start.55
  502.3 46.9 %copy-start.5 = (bf16[512,768]{1,0:T(8,128)(2,1)S(1)}, bf16[512,768]{1,0:T(8,128)(2,1)}, u32[]{:S(2)}) copy-start(bf16[512,768]{1,0:T(8,128)(2,1)} %param.12) | copy-start | bytes 2359300
  504.2 46.9 %copy-start.57 = (f32[512]{0:T(512)S(1)}, f32[512]{0:T(512)}, u32[]{:S(2)}) copy-start(f32[512]{0:T(512)} %copy-done.56) | copy-start | bytes 6148
  506.7 173.8 %copy-start.7 = (f32[512,768]{1,0:T(8,128)S(1)}, f32[512,768]{1,0:T(8,128)}, u32[]{:S(2)}) copy-start(f32[512,768]{1,0:T(8,128)} %copy-done.6) | copy-start | bytes 4718596
  678.9 4.0 copy-start.1
  (33 other events, 40.5 us)
Sparse Core Ops, SparseCore 0:
  57.9 46.8 all-reduce.9
  334.5 48.1 all-reduce.15
  397.0 105.1 all-reduce.13
  505.1 44.0 all-reduce.11
where the time goes:
time: 700 us; the launch traced here: 690 us
  local copies, waits for them, and re-layouts  252 us (36%)
  waiting for transfers between devices  211 us (30%)
  blocking collectives  127 us (18%)
  matrix products  38 us (5%)
  other arithmetic  23.6 us (3%)
  starting transfers between devices  23.4 us (3%)
  between operations  14.8 us (2%)
    psum x1, blocking collectives, local(): lax.psum(grad_bias.astype(jnp.bfloat16), 'expert').astype(jnp.float32)  127 us
    scatter x1, local copies, waits for them, and re-layouts, local(): outgoing = empty_rows.at[route, slot].set(mixed_b).reshape(owners, expert...  67.8 us
    scatter x1, local copies, waits for them, and re-layouts, local(): back_out = empty_rows.at[route, slot].set(grad_expert).reshape(owners, ex...  67.8 us
    psum x1, waiting for transfers between devices, return_home(): summed = lax.psum(by_expert[route, slot].astype(jnp.bfloat16), 'shard')  47.7 us
    psum x1, waiting for transfers between devices, local(): lax.psum(jnp.dot(heads_out, out_proj, preferred_element_type=jnp.float32)...  47 us
    psum x1, waiting for transfers between devices, local(): lax.psum(jnp.einsum('cte,cde->td', grad_proj, qkv_weight, preferred_eleme...  42.4 us
    unnamed x153, local copies, waits for them, and re-layouts  41.2 us
    psum x1, waiting for transfers between devices, local(): lax.psum(grad_qkv.astype(jnp.bfloat16), 'expert').astype(jnp.float32)  40.8 us
  transfers between devices with their start and end apart: 8, of which 7 were waited for; matrix products, arithmetic and copies ran while one was open for 23% of the time, Pallas kernels for 0%

commit v1 on v0

v1 whole, which is shorter than its diff:
```python
import jax
import jax.numpy as jnp
from jax import lax
from jax.experimental import pallas as pl
from jax.experimental.pallas import tpu as pltpu
from jax.sharding import PartitionSpec as P

EPS = 1e-06
T = 512
D = 768
NH = 3
HD = 64
W = NH * HD
NE = 32
CAP = 24
SLOTS = NE * CAP
NS = 4
SCALE = HD ** (-0.5)
f32 = jnp.float32
b16 = jnp.bfloat16

NN = (((1,), (0,)), ((), ()))
NT = (((1,), (1,)), ((), ()))
TN = (((0,), (0,)), ((), ()))


def dot(a, b, dims=NN):
    return lax.dot_general(a, b, dims, preferred_element_type=f32)


def call(body, outs, *args, name, flops=0, smem=(), scratch=(), grid=None, in_specs=None, out_specs=None):
    outs = [jax.ShapeDtypeStruct(s, t) for s, t in outs]
    if in_specs is None:
        in_specs = [
            pl.BlockSpec(memory_space=pltpu.SMEM if i in smem else pltpu.VMEM) for i in range(len(args))
        ]
        out_specs = [pl.BlockSpec(memory_space=pltpu.VMEM) for _ in outs]
    size = sum(a.size * a.dtype.itemsize for a in args) + sum(o.size * o.dtype.itemsize for o in outs)
    return pl.pallas_call(
        body,
        out_shape=outs,
        grid=grid or (),
        in_specs=in_specs,
        out_specs=out_specs,
        scratch_shapes=list(scratch),
        compiler_params=pltpu.CompilerParams(vmem_limit_bytes=48 * 1024 * 1024),
        cost_estimate=pl.CostEstimate(flops=flops, bytes_accessed=size, transcendentals=0),
        name=name,
    )(*args)


def lanes(shape):
    return lax.broadcasted_iota(jnp.int32, shape, len(shape) - 1)


def rows_of(shape):
    return lax.broadcasted_iota(jnp.int32, shape, len(shape) - 2)


def roll_half(v):
    return pltpu.roll(v, 64, v.ndim - 1)


def inv_rms(v):
    return lax.rsqrt(jnp.mean(v * v, axis=-1, keepdims=True) + EPS)


def toeplitz_rows(offsets_row, rows, shift):
    wide = jnp.broadcast_to(offsets_row, (rows, offsets_row.shape[1]))
    return pltpu.roll(wide, shift, 1, stride=1, stride_axis=0)


def bucket_hot(bk):
    return (bk == rows_of((NE, 1024))).astype(f32)


def pack_rows(block, half):
    low = lanes((T // 2, 128)) < 64
    tail = jnp.where(low, half[: T // 2], roll_half(half[T // 2 :]))
    return jnp.concatenate([block, tail], axis=0).astype(b16)


def unpack_rows(pieces):
    low = lanes((T // 2, 128)) < 64
    blocks = [p[:T] for p in pieces]
    for left, right in ((0, 1), (2, 3)):
        l_half = pieces[left][T:].astype(f32)
        r_half = pieces[right][T:].astype(f32)
        top = jnp.where(low, l_half, roll_half(r_half))
        bottom = jnp.where(low, roll_half(l_half), r_half)
        blocks.append(jnp.concatenate([top, bottom], axis=0).astype(b16))
    return jnp.concatenate(blocks, axis=1)


def order_pieces(me, refs, held):
    for d, ref in enumerate(refs):
        held[pl.ds(lax.rem(me + (NS - d), NS), 1)] = ref[...][None]


def dispatch_body(idx, val, out):
    hot = (idx[...] == rows_of((SLOTS, T))).astype(b16)
    out[...] = dot(hot, val[...]).reshape(NE, CAP, D).astype(b16)


def attend_body(tok, gains, w, rb, bk, heads, heads_t, a_out, qk_t, v_out, p_out):
    x = tok[...].astype(f32)
    a = (x * inv_rms(x) * gains[0:1, :]).astype(b16)
    a_out[...] = a
    q = dot(a, w[0])
    k = dot(a, w[1])
    v = dot(a, w[2])
    q_t = q.T.astype(b16)
    k_t = k.T.astype(b16)
    v_t = v.T.astype(b16)
    k = k.astype(b16)
    qk_t[0] = q_t
    qk_t[1] = k_t
    v_out[...] = v.astype(b16)
    off = lax.dot_general(rb[...], bucket_hot(bk[...]), NN, precision=lax.Precision.HIGHEST, preferred_element_type=f32)
    outs = []
    for h in range(NH):
        part = slice(HD * h, HD * h + HD)
        s = dot(k[:, part], q_t[part]) * SCALE
        wide = toeplitz_rows(off[h : h + 1], 128, 897)
        bias = jnp.concatenate([wide[:, 384 - 128 * b : 896 - 128 * b] for b in range(4)], axis=0)
        s = s + bias
        e = jnp.exp(s - jnp.max(s, axis=0, keepdims=True))
        p = e / jnp.sum(e, axis=0, keepdims=True)
        p_out[h] = p
        outs.append(dot(v_t[part], p.astype(b16)))
    heads_t[...] = jnp.concatenate(outs, axis=0).astype(b16)
    block = jnp.concatenate(outs[:2], axis=0).T
    tail = jnp.concatenate([outs[2][:, : T // 2], outs[2][:, T // 2 :]], axis=0).T
    heads[...] = jnp.concatenate([block, tail], axis=0).astype(b16)


def order_weights_body(me, w0, w1, w2, w3, out, held):
    order_pieces(me[0], (w0, w1, w2, w3), held)
    parts = [held[j, :128] for j in range(NS)] + [held[j, 128:] for j in range(NS)]
    out[...] = jnp.concatenate(parts, axis=0)


def mix_body(me, idx, tok, gains, h0, h1, h2, h3, w, rows, u_out, hidden_out, held):
    order_pieces(me[0], (h0, h1, h2, h3), held)
    full = unpack_rows([held[j] for j in range(NS)])
    hidden = tok[...].astype(f32) + dot(full, w[...])
    u = (hidden * inv_rms(hidden) * gains[1:2, :]).astype(b16)
    hot = (idx[...] == rows_of((SLOTS, T))).astype(b16)
    rows[...] = dot(hot, u).reshape(NE, CAP, D).astype(b16)
    u_out[...] = u
    hidden_out[...] = hidden


def gate_body(u, router, route, gate_out, coef_out, coef_router_out):
    logits = dot(u[...], router[...])
    e = jnp.exp(logits - jnp.max(logits, axis=1, keepdims=True))
    probs = e / jnp.sum(e, axis=1, keepdims=True)
    chosen = (route[...] == lanes((T, NE))).astype(f32)
    gate = jnp.sum(probs * chosen, axis=1, keepdims=True)
    coef = probs * (chosen - gate)
    high = coef.astype(b16)
    low = (coef - high.astype(f32)).astype(b16)
    gate_out[...] = gate
    coef_out[...] = coef
    coef_router_out[...] = dot(high, router[...], NT) + dot(low, router[...], NT)


def ungated_body(g, w_out, h):
    h[...] = dot(g[...], w_out[...], NT)


def pack_return(val, extra, out):
    n = val.shape[0] // CAP
    low = lanes((n, 8, 128)) < 64
    if extra is not None:
        ext = extra.reshape(n, CAP, 1)
        hi = ext.astype(b16).astype(f32)
        lo = ext - hi
        lane = lanes((n, 8, 128))
        tail = jnp.zeros((n, 8, 128), f32)
        for t in range(3):
            tail = jnp.where(lane == 64 + t, hi[:, 8 * t : 8 * t + 8], tail)
            tail = jnp.where(lane == 67 + t, lo[:, 8 * t : 8 * t + 8], tail)
    else:
        tail = jnp.zeros((n, 8, 128), f32)
    res = []
    for s in range(NS):
        block = val[:, 128 * s : 128 * s + 128].reshape(n, CAP, 128)
        c = 512 + 128 * (s // 2)
        half = val[:, c : c + 128].reshape(n, CAP, 128)
        moved = roll_half(half)
        x0, x1, x2 = (half[:, 8 * t : 8 * t + 8] for t in range(3))
        r0, r1, r2 = (moved[:, 8 * t : 8 * t + 8] for t in range(3))
        if s % 2 == 0:
            t3, t4 = jnp.where(low, x0, r1), jnp.where(low, x2, tail)
        else:
            t3, t4 = jnp.where(low, r0, x1), jnp.where(low, r2, tail)
        res.append(jnp.concatenate([block, t3, t4], axis=1))
    out[...] = jnp.stack(res, axis=1).astype(b16)


GELU_C = 0.7978845608028654


def expert_body(me, rows, h, w_in, router, ret, act_out, dpre_out, gate_out):
    u = rows[...]
    logits = dot(u, router[...])
    e = jnp.exp(logits - jnp.max(logits, axis=1, keepdims=True))
    mine = (lanes(logits.shape) == me[0]).astype(f32)
    gate = jnp.sum(e * mine, axis=1, keepdims=True) / jnp.sum(e, axis=1, keepdims=True)
    pre = dot(u, w_in[...])
    sq = pre * pre
    th = jnp.tanh(GELU_C * pre * (1.0 + 0.044715 * sq))
    act = (0.5 * pre * (1.0 + th)).astype(b16)
    slope = 0.5 * (1.0 + th) + 0.5 * pre * (1.0 - th * th) * (GELU_C * (1.0 + 3 * 0.044715 * sq))
    hv = h[...]
    d_gate = jnp.sum(act.astype(f32) * hv, axis=1, keepdims=True)
    d_pre = (gate * hv * slope).astype(b16)
    act_out[...] = act
    dpre_out[...] = d_pre
    gate_out[...] = gate
    pack_return(dot(d_pre, w_in[...], NT), d_gate, ret)


def value_body(act, w_out, ret):
    pack_return(dot(act[...], w_out[...]), None, ret)


def collect_body(idx, got, piece, *d_gate):
    total = jnp.sum(got[...].astype(f32), axis=1)
    block = total[:, :CAP].reshape(SLOTS, 128).astype(b16)
    t3 = total[:, 24:32]
    t4 = total[:, 32:40]
    half = jnp.concatenate([t3, roll_half(t3), t4], axis=1).reshape(SLOTS, 128)
    lane = lanes((SLOTS, 128))
    if d_gate:
        tl = lanes(t4.shape)
        cols = []
        for t in range(3):
            cols.append(jnp.sum(jnp.where((tl == 64 + t) | (tl == 67 + t), t4, 0.0), axis=2, keepdims=True))
        col = jnp.concatenate(cols, axis=1).reshape(SLOTS, 1)
        hi = col.astype(b16).astype(f32)
        half = jnp.where(lane < 64, half, jnp.where(lane == 64, hi, jnp.where(lane == 65, col - hi, 0.0)))
    else:
        half = jnp.where(lane < 64, half, 0.0)
    hot = (idx[...] == lanes((T, SLOTS))).astype(b16)
    mine = dot(hot, jnp.concatenate([block, half.astype(b16)], axis=1))
    piece[...] = pack_rows(mine[:, :128], mine[:, 128:])
    if d_gate:
        lt = lanes((T, 128))
        d_gate[0][...] = jnp.sum(
            jnp.where((lt == 64) | (lt == 65), mine[:, 128:], 0.0), axis=1, keepdims=True
        )


def backward_body(
    me, p0, p1, p2, p3, d_gate, coef, coef_router, u, cot, hidden_in, gains, out_proj, heads_t, a, qk_t, v, p, w, bk,
    pay, da_out, dhid_out, held, scr,
):
    order_pieces(me[0], (p0, p1, p2, p3), held)
    d_expert = unpack_rows([held[j] for j in range(NS)]).astype(f32)
    dg = d_gate[...]
    d_u = dg * coef_router[...] + d_expert
    hidden = hidden_in[...]
    r2 = inv_rms(hidden)
    n2 = hidden * r2
    gain_two = jnp.sum(d_u * n2, axis=0, keepdims=True)
    v2 = d_u * gains[1:2, :]
    d_hidden = cot[...].astype(f32) + r2 * (v2 - n2 * jnp.mean(v2 * n2, axis=-1, keepdims=True))
    dhid_out[...] = d_hidden
    d_att = d_hidden.astype(b16)
    d_logits = coef[...] * dg
    high = d_logits.astype(b16)
    low = (d_logits - high.astype(f32)).astype(b16)
    router_t = dot(high, u[...], TN) + dot(low, u[...], TN)
    g_out = dot(heads_t[...], d_att)
    do_t = dot(out_proj[...], d_att, NT).astype(b16)
    hot = bucket_hot(bk[...])
    dqs, dks, dvs, bias = [], [], [], []
    for h in range(NH):
        part = slice(HD * h, HD * h + HD)
        prob = p[h]
        dp = dot(v[:, part], do_t[part])
        delta = jnp.sum(prob * dp, axis=0, keepdims=True)
        ds = (prob * (dp - delta)).astype(b16)
        dvs.append(dot(do_t[part], prob.astype(b16), NT))
        dks.append(dot(qk_t[0, part], ds, NT) * SCALE)
        dqs.append(dot(qk_t[1, part], ds) * SCALE)
        ds_f = ds.astype(f32)
        acc = jnp.zeros((128, 1024), f32)
        for b in range(4):
            left, right = 384 - 128 * b, 128 + 128 * b
            blk = ds_f[128 * b : 128 * b + 128]
            parts = ([jnp.zeros((128, left), f32)] if left else []) + [blk, jnp.zeros((128, right), f32)]
            acc = acc + jnp.concatenate(parts, axis=1)
        acc = pltpu.roll(acc, 127, 1)
        row = rows_of((128, 1024))
        for bit in range(7):
            step = 1 << bit
            acc = jnp.where((row & step) != 0, pltpu.roll(acc, 1024 - step, 1), acc)
        bias.append(jnp.sum(acc, axis=0, keepdims=True))
    bias = lax.dot_general(
        jnp.concatenate(bias + [jnp.zeros((5, 1024), f32)], axis=0), hot, NT,
        precision=lax.Precision.HIGHEST, preferred_element_type=f32,
    )
    dq = jnp.concatenate(dqs, axis=0).astype(b16)
    dk = jnp.concatenate(dks, axis=0).astype(b16)
    dv = jnp.concatenate(dvs, axis=0).astype(b16)
    da = dot(w[0], dq) + dot(w[1], dk) + dot(w[2], dv)
    a_v = a[...]
    grads = [dot(m, a_v) for m in (dq, dk, dv)]
    gain_rows = [
        jnp.sum(w[c].astype(f32).T * grads[c], axis=0, keepdims=True) for c in range(3)
    ]
    gain_one = gain_rows[0] + gain_rows[1] + gain_rows[2]
    full = jnp.concatenate(grads + [g_out], axis=0)
    for l in range(6):
        cut = slice(128 * l, 128 * l + 128)
        scr[:, 24 * l : 24 * l + 24, :] = full[:, cut].reshape(NE, CAP, 128)
        scr[:, 144 + l, :] = router_t[:, cut]
    scr[:, 150:152, :] = jnp.zeros((NE, 2, 128), f32)
    for l in range(6):
        scr[l, 150:151, :] = gain_two[:, 128 * l : 128 * l + 128]
    wide = jnp.concatenate([bias, jnp.zeros((8, 96), f32)], axis=1)
    for h in range(NH):
        scr[6 + h, 150:151, :] = wide[h : h + 1]
    pay[...] = scr[...].astype(b16)
    gl = jnp.concatenate(
        [gain_one[:, 128 * l : 128 * l + 128] for l in range(6)] + [jnp.zeros((2, 128), f32)], axis=0
    )
    hi = gl.astype(b16).astype(f32)
    gl = jnp.concatenate([hi, gl - hi], axis=0)
    for s in range(NS):
        da_out[s] = jnp.concatenate([da[:, 128 * s : 128 * s + 128], gl], axis=0).astype(b16)


def sum_body(pay, da, out):
    total = jnp.sum(pay[...].astype(f32), axis=0)
    gl = jnp.sum(da[:, D:, :].astype(f32), axis=0)
    chunk = jnp.concatenate([total, gl[:8] + gl[8:]], axis=0).astype(b16)
    out[...] = jnp.broadcast_to(chunk[None], (NE, 160, 128))


def token_grad_body(me, da, tok, dhid, gains, out):
    d_a = jnp.sum(da[:, :D, :].astype(f32), axis=0).T
    at = pl.ds(pl.multiple_of(me[0] * 128, 128), 128)
    x = tok[at, :].astype(f32)
    r1 = inv_rms(x)
    n1 = x * r1
    v1 = d_a * gains[0:1, :]
    out[...] = (dhid[at, :] + r1 * (v1 - n1 * jnp.mean(v1 * n1, axis=-1, keepdims=True))).astype(b16)


def join_body(me, t0, t1, t2, t3, out):
    for d, ref in enumerate((t0, t1, t2, t3)):
        src = lax.rem(me[0] + (NS - d), NS)
        out[pl.ds(pl.multiple_of(src * 128, 128), 128), :] = ref[...]


def result_body(me, p0, p1, p2, p3, gate, hidden, out, held):
    order_pieces(me[0], (p0, p1, p2, p3), held)
    value = unpack_rows([held[j] for j in range(NS)]).astype(f32)
    out[...] = (hidden[...] + gate[...] * value).astype(b16)


def finish_body(got, gains, qkv, proj, bias, gains_out, router, scr):
    scr[...] = got[...].astype(f32)
    full = jnp.concatenate([scr[:, 24 * l : 24 * l + 24, :].reshape(D, 128) for l in range(6)], axis=1)
    for c in range(3):
        qkv[c] = full[W * c : W * c + W].T
    proj[...] = full[3 * W :]
    router[...] = jnp.concatenate([scr[:, 144 + l, :] for l in range(6)], axis=1).T
    gl = jnp.sum(scr[:, 152:160, :], axis=0)
    one = jnp.concatenate([gl[l : l + 1] for l in range(6)], axis=1) / gains[0:1, :]
    two = jnp.concatenate([scr[l, 150:151, :] for l in range(6)], axis=1)
    gains_out[...] = jnp.concatenate([one, two], axis=0)
    bias[...] = jnp.concatenate([scr[6 + h, 150:151, :NE] for h in range(NH)], axis=0)


def over_experts(v):
    return lax.all_to_all(v, "expert", split_axis=0, concat_axis=0, tiled=True)


def over_all(v):
    return lax.all_to_all(v, ("expert", "shard"), split_axis=0, concat_axis=0, tiled=True)


def round_shard(v):
    return [v] + [lax.ppermute(v, "shard", [(i, (i + d) % NS) for i in range(NS)]) for d in (1, 2, 3)]


def local(tokens, qkv_weight, out_proj, rel_bias, gains, router, w_in, w_out, route, slot, buckets, cotangent):
    w_in = w_in.reshape(D, -1)
    w_out = w_out.reshape(-1, D)
    ff = w_in.shape[1]
    me = jnp.full((1,), lax.axis_index("shard"), jnp.int32)
    expert = jnp.full((1,), lax.axis_index("expert"), jnp.int32)
    idx = route * CAP + slot
    idx_row = idx[None, :]
    idx_col = idx[:, None]
    bk = jnp.concatenate([jnp.flip(buckets), jnp.full((1,), -1, jnp.int32)])[None, :]

    (g_rows,) = call(dispatch_body, [((NE, CAP, D), b16)], idx_row, cotangent, name="dispatch_cotangent")
    g_rows = over_experts(g_rows).reshape(SLOTS, D)
    w_pieces = round_shard(out_proj)

    heads, heads_t, a, qk_t, v, p = call(
        attend_body,
        [((D, 128), b16), ((W, T), b16), ((T, D), b16), ((2, W, T), b16), ((T, W), b16), ((NH, T, T), f32)],
        tokens, gains, qkv_weight, rel_bias, bk, name="attend",
    )
    h_pieces = round_shard(heads)
    (w_full,) = call(
        order_weights_body, [((D, D), b16)], me, *w_pieces, name="order_weights", smem=(0,),
        scratch=[pltpu.VMEM((NS, W, D), b16)],
    )
    (h,) = call(ungated_body, [((SLOTS, ff), f32)], g_rows, w_out, name="ungated")
    rows, u, hidden = call(
        mix_body,
        [((NE, CAP, D), b16), ((T, D), b16), ((T, D), f32)],
        me, idx_row, tokens, gains, *h_pieces, w_full, name="mix", smem=(0,),
        scratch=[pltpu.VMEM((NS, D, 128), b16)],
    )
    u_rows = over_experts(rows).reshape(SLOTS, D)
    gate, coef, coef_router = call(
        gate_body, [((T, 1), f32), ((T, NE), f32), ((T, D), f32)], u, router, route[:, None], name="gate",
    )
    half = SLOTS // 2
    vm = pltpu.VMEM
    row_spec = lambda n: pl.BlockSpec((half, n), lambda i: (i, 0), memory_space=vm)
    all_spec = lambda s: pl.BlockSpec(s, lambda i: (0,) * len(s), memory_space=vm)
    ret_spec = pl.BlockSpec((NE // 2, NS, 40, 128), lambda i: (i, 0, 0, 0), memory_space=vm)
    ret, act, d_pre, row_gate = call(
        expert_body,
        [((NE, NS, 40, 128), b16), ((SLOTS, ff), b16), ((SLOTS, ff), b16), ((SLOTS, 1), f32)],
        expert, u_rows, h, w_in, router, name="expert", grid=(2,),
        in_specs=[pl.BlockSpec(memory_space=pltpu.SMEM), row_spec(D), row_spec(ff), all_spec((D, ff)), all_spec((D, NE))],
        out_specs=[ret_spec, row_spec(ff), row_spec(ff), row_spec(1)],
    )
    back = over_all(ret.reshape(NE * NS, 40, 128)).reshape(NE, NS, 40, 128)
    (val,) = call(
        value_body, [((NE, NS, 40, 128), b16)], act, w_out, name="value", grid=(2,),
        in_specs=[row_spec(ff), all_spec((ff, D))], out_specs=[ret_spec],
    )
    piece, d_gate = call(
        collect_body, [((D, 128), b16), ((T, 1), f32)], idx_col, back, name="collect_back"
    )
    b_pieces = round_shard(piece)
    value = over_all(val.reshape(NE * NS, 40, 128)).reshape(NE, NS, 40, 128)
    d_rows = (row_gate * g_rows.astype(f32)).astype(b16)
    grad_w_out = dot(act, d_rows, TN)[None]
    grad_w_in = dot(u_rows, d_pre, TN)[None]

    pay, da, d_hidden = call(
        backward_body,
        [((NE, 152, 128), b16), ((NS, D + 16, 128), b16), ((T, D), f32)],
        me, *b_pieces, d_gate, coef, coef_router, u, cotangent, hidden, gains, out_proj, heads_t, a, qk_t, v, p,
        qkv_weight, bk, name="backward", smem=(0,),
        scratch=[pltpu.VMEM((NS, D, 128), b16), pltpu.VMEM((NE, 152, 128), f32)],
    )
    pay = over_experts(pay)
    da = lax.all_to_all(da, "shard", split_axis=0, concat_axis=0, tiled=True)
    (chunk,) = call(sum_body, [((NE, 160, 128), b16)], pay, da, name="sum_gradients")
    chunk = over_experts(chunk)
    (t_piece,) = call(token_grad_body, [((128, D), b16)], me, da, tokens, d_hidden, gains, name="token_grad", smem=(0,))
    (grad_tokens,) = call(join_body, [((T, D), b16)], me, *round_shard(t_piece), name="join_tokens", smem=(0,))
    (v_piece,) = call(collect_body, [((D, 128), b16)], idx_col, value, name="collect_value")
    (result,) = call(
        result_body, [((T, D), b16)], me, *round_shard(v_piece), gate, hidden, name="result", smem=(0,),
        scratch=[pltpu.VMEM((NS, D, 128), b16)],
    )
    grad_qkv, grad_proj, grad_bias, grad_gains, grad_router = call(
        finish_body,
        [((3, D, W), f32), ((W, D), f32), ((NH, NE), f32), ((2, D), f32), ((D, NE), f32)],
        chunk, gains, name="finish", scratch=[pltpu.VMEM((NE, 160, 128), f32)],
    )
    return result, grad_tokens, grad_qkv, grad_proj, grad_bias, grad_gains, grad_router, grad_w_in, grad_w_out


def solution(mesh):
    in_specs = (
        P("expert", None),
        P(None, None, "shard"),
        P("shard", None),
        P("shard", None),
        P(),
        P(),
        P("expert", None, "shard"),
        P("expert", "shard", None),
        P("expert"),
        P("expert"),
        P(),
        P("expert", None),
    )
    out_specs = (
        P("expert", None),
        P("expert", None),
        P(None, None, "shard"),
        P("shard", None),
        P("shard", None),
        P(),
        P(),
        P("expert", None, "shard"),
        P("expert", "shard", None),
    )
    return jax.shard_map(local, mesh=mesh, in_specs=in_specs, out_specs=out_specs, check_vma=False)
```

time: 700 us -> 250 us (0.36); the launches traced: 690 us -> 249 us
  local copies, waits for them, and re-layouts: 252 us -> 36.7 us
  waiting for transfers between devices: 211 us -> 90.7 us
  blocking collectives: 127 us -> 15.3 us
  Pallas kernels: 0 us -> 41.2 us
  starting transfers between devices: 23.4 us -> 56.1 us
  matrix products: 38 us -> 6.41 us
  other arithmetic: 23.6 us -> 1.55 us
  between operations: 14.8 us -> 0.99 us
    psum x4 -> x0, waiting for transfers between devices: 178 us -> none  [the longest x1 47.7 us: return_home(): summed = lax.psum(by_expert[route, slot].astype(jnp.bfloat16), 'shard')]
    scatter x2 -> x0, local copies, waits for them, and re-layouts: 136 us -> none  [the longest x1 67.8 us: local(): outgoing = empty_rows.at[route, slot].set(mixed_b).reshape(owners, expert...]
    psum x1 -> x0, blocking collectives: 127 us -> none  [local(): lax.psum(grad_bias.astype(jnp.bfloat16), 'expert').astype(jnp.float32)]
    pallas_call x0 -> x16, Pallas kernels: none -> 41.2 us  [call(): pl.pallas_call(body, out_shape=outs, grid=grid or (), in_specs=in_specs,...]
    all_to_all x4 -> x6, waiting for transfers between devices: 33.3 us -> 69.4 us  [the longest x2 40.7 us: over_all(): lax.all_to_all(v, ('expert', 'shard'), split_axis=0, concat_axis=0, tiled...]
    dot_general x22 -> x2, matrix products: 35.9 us -> 6.41 us  [dot(): return lax.dot_general(a, b, dims, preferred_element_type=f32)]
    reshape x4 -> x0, local copies, waits for them, and re-layouts: 26.5 us -> none  [the longest x1 13.3 us: diagonal_sums(): skewed = flat.reshape(heads_local, row_block, skew_width - 1)]
    ppermute x0 -> x15, starting transfers between devices: none -> 21.5 us  [round_shard(): lax.ppermute(v, 'shard', [(i, (i + d) % NS) for i in range(NS)])]
  transfers between devices with their start and end apart: 8 -> 21, of which waited for: 7 -> 13; matrix products, arithmetic and copies ran while one was open for 23% -> 4% of each run, Pallas kernels for 0% -> 8%
where the time goes in v1:
time: 250 us; the launch traced here: 249 us
  waiting for transfers between devices  90.7 us (36%)
  starting transfers between devices  56.1 us (22%)
  Pallas kernels  41.2 us (16%)
  local copies, waits for them, and re-layouts  36.7 us (15%)
  blocking collectives  15.3 us (6%)
  matrix products  6.41 us (3%)
    pallas_call x16, Pallas kernels, call(): pl.pallas_call(body, out_shape=outs, grid=grid or (), in_specs=in_specs,...  41.2 us
    all_to_all x2, waiting for transfers between devices, over_all(): lax.all_to_all(v, ('expert', 'shard'), split_axis=0, concat_axis=0, tiled...  40.7 us
    unnamed x110, local copies, waits for them, and re-layouts  36.4 us
    all_to_all x4, waiting for transfers between devices, over_experts(): return lax.all_to_all(v, 'expert', split_axis=0, concat_axis=0, tiled=True)  28.7 us
    all_to_all x4, starting transfers between devices, over_experts(): return lax.all_to_all(v, 'expert', split_axis=0, concat_axis=0, tiled=True)  23.9 us
    ppermute x15, starting transfers between devices, round_shard(): lax.ppermute(v, 'shard', [(i, (i + d) % NS) for i in range(NS)])  21.5 us
    ppermute x15, waiting for transfers between devices, round_shard(): lax.ppermute(v, 'shard', [(i, (i + d) % NS) for i in range(NS)])  21.2 us
    all_to_all x1, blocking collectives, local(): da = lax.all_to_all(da, 'shard', split_axis=0, concat_axis=0, tiled=True)  15.3 us
  transfers between devices with their start and end apart: 21, of which 13 were waited for; matrix products, arithmetic and copies ran while one was open for 4% of the time, Pallas kernels for 8%

profile of v1, /device:TPU:0, one launch (start us, length us, event | category | flops | bytes accessed | tf_op | source)
XLA Modules:
  0.0 248.9 jit_solution(4144282247374521702)
XLA Ops:
  2.5 1.8 dispatch_cotangent.1
  4.3 8.4 %all-to-all-start.1 = ((bf16[32,24,768]{2,1,0:T(8,128)(2,1)}), bf16[32,24,768]{2,1,0:T(8,128)(2,1)S(1)}, u32[]{:S(2)}, u32[]{:S(2)}) async-start(bf16[32,24,768]{2,1,0:T(8,128)(2,1)} %dispatch_cotangent.1), calls=%async_computation.1 | async-start | bytes 2359296 | tf_op jit(solution)/shard_map/all_to_all | solution.py:381
  12.7 1.6 collective-permute-start.3
  14.4 2.9 %collective-permute-start.4 = (bf16[192,768]{1,0:T(8,128)(2,1)S(1)}, bf16[192,768]{1,0:T(8,128)(2,1)}, u32[]{:S(2)}, u32[]{:S(2)}) collective-permute-start(bf16[192,768]{1,0:T(8,128)(2,1)S(1)} %copy-done.23), channel_id=1, source_target_pairs={{0,2},{1,3},{2,0},{3,1},{4,6},{5,7},{6,4},{7,5},{8,10},{9,11},{10,... | collective-permute-start | bytes 884744 | tf_op jit(solution)/shard_map/ppermute | solution.py:389
  17.3 1.3 collective-permute-start.5
  18.6 1.5 copy.27.w
  20.4 4.5 %attend.1 = (bf16[768,128]{1,0:T(8,128)(2,1)}, bf16[192,512]{1,0:T(8,128)(2,1)S(1)}, bf16[512,768]{1,0:T(8,128)(2,1)S(1)}, bf16[2,192,512]{2,1,0:T(8,128)(2,1)S(...) custom-call(bf16[512,768]{1,0:T(8,128)(2,1)S(1)} %copy-done.2, f32[2,768]{1,0:T(2,128)S(1)} %copy-done.43, ...), custom_call_target="tpu_custom_call" | custom-call | bytes 6596992 | tf_op jit(solution)/shard_map/attend/pallas_call | solution.py:39
  29.4 1.9 collective-permute-start.2
  31.5 1.3 order_weights.1.w
  32.8 7.1 %collective-permute-done.h1 = bf16[768,128]{1,0:T(8,128)(2,1)} collective-permute-done((bf16[768,128]{1,0:T(8,128)(2,1)}, bf16[768,128]{1,0:T(8,128)(2,1)}, u32[]{:S(2)}, u32[]{:S(2)}) %collective-permute-start) | collective-permute-done | bytes 196640 | tf_op jit(solution)/shard_map/ppermute | solution.py:389
  40.5 3.9 %mix.1 = (bf16[32,24,768]{2,1,0:T(8,128)(2,1)S(1)}, bf16[512,768]{1,0:T(8,128)(2,1)S(1)}, f32[512,768]{1,0:T(8,128)}) custom-call(s32[1]{0:T(128)} %bitcast.me, s32[1,512]{1,0:T(1,128)S(1)} %bitcast.34, bf16[512,768]{1,0:T(8,128)(2,1)S(1)} %copy-done.2, f32[2,768]{1,0:T(2,128)S(1)} %copy-done.43, bf16[768,128]{1,0:T(8,128)(2,1)} %get-tuple-element.35.h0, ...), custom_call_target="tpu_custom_call" | custom-call | bytes 6299652 | tf_op jit(solution)/shard_map/mix/pallas_call | solution.py:39
  47.4 7.4 %all-to-all-start = ((bf16[32,24,768]{2,1,0:T(8,128)(2,1)}), bf16[32,24,768]{2,1,0:T(8,128)(2,1)S(1)}, u32[]{:S(2)}, u32[]{:S(2)}) async-start(bf16[32,24,768]{2,1,0:T(8,128)(2,1)} %copy-done.28), calls=%async_computation | async-start | bytes 2359296 | tf_op jit(solution)/shard_map/all_to_all | solution.py:381
  55.0 1.3 copy-done.13
  57.4 1.4 copy-done.1
  58.8 14.4 %all-to-all-done = bf16[32,24,768]{2,1,0:T(8,128)(2,1)S(1)} async-done(((bf16[32,24,768]{2,1,0:T(8,128)(2,1)}), bf16[32,24,768]{2,1,0:T(8,128)(2,1)S(1)}, u32[]{:S(2)}, u32[]{:S(2)}) %all-to-all-start) | async-done | bytes 1179680 | tf_op jit(solution)/shard_map/all_to_all | solution.py:381
  73.2 1.7 copy-done.25
  74.8 6.3 %expert.1 = (bf16[32,4,40,128]{3,2,1,0:T(8,128)(2,1)}, bf16[768,768]{1,0:T(8,128)(2,1)S(1)}, bf16[768,768]{1,0:T(8,128)(2,1)S(1)}, f32[768,1]{1,0:T(8,128)S(1)}) custom-call(s32[1]{0:T(128)} %bitcast.2.me, bf16[768,768]{1,0:T(8,128)(2,1)S(1)} %bitcast.24, f32[768,768]{1,0:T(8,128)} %copy-done.1, bf16[768,768]{1,0:T(8,128)(2,1)S(1)} %bitcast.30, ...), custom_call_target="tpu_custom_call" | custom-call | bytes 8440836 | tf_op jit(solution)/shard_map/expert/pallas_call | solution.py:39
  84.0 6.1 %all-to-all-start.3 = ((bf16[128,40,128]{2,1,0:T(8,128)(2,1)}), bf16[128,40,128]{2,1,0:T(8,128)(2,1)S(1)}, u32[]{:S(2)}, u32[]{:S(2)}) async-start(bf16[128,40,128]{2,1,0:T(8,128)(2,1)} %bitcast.36), calls=%async_computation.3 | async-start | bytes 2621440 | tf_op jit(solution)/shard_map/all_to_all | solution.py:385
  90.2 21.6 %all-to-all-done.3 = bf16[128,40,128]{2,1,0:T(8,128)(2,1)S(1)} async-done(((bf16[128,40,128]{2,1,0:T(8,128)(2,1)}), bf16[128,40,128]{2,1,0:T(8,128)(2,1)S(1)}, u32[]{:S(2)}, u32[]{:S(2)}) %all-to-all-start.3) | async-done | bytes 1310752 | tf_op jit(solution)/shard_map/all_to_all | solution.py:385
  111.8 1.7 collect_back.1
  115.0 2.4 collective-permute-start.11
  118.8 1.7 gate.1
  122.3 1.3 collective-permute-done.10.p2
  123.6 1.6 collective-permute-done.11.p3
  125.2 2.0 collective-permute-done.9.p1
  131.4 11.0 %backward.1 = (bf16[32,152,128]{2,1,0:T(8,128)(2,1)}, bf16[4,784,128]{2,1,0:T(8,128)(2,1)S(1)}, f32[512,768]{1,0:T(8,128)}) custom-call(s32[1]{0:T(128)} %bitcast.me, bf16[768,128]{1,0:T(8,128)(2,1)} %get-tuple-element.42.p0, bf16[768,128]{1,0:T(8,128)(2,1)S(1)} %collective-permute-done.9.p1, bf16[768,128]{1,0:T(8,128)(2,1)S(1)} %collective-permute-done.10.p2, ...), custom_call_target="tpu_custom_call" | custom-call | bytes 15101956 | tf_op jit(solution)/shard_map/backward/pallas_call | solution.py:39
  142.4 15.3 %all_to_all.35.da = bf16[4,784,128]{2,1,0:T(8,128)(2,1)S(1)} all-to-all(bf16[4,784,128]{2,1,0:T(8,128)(2,1)S(1)} %get-tuple-element.51), channel_id=1, replica_groups=mesh['expert'=32,'shard'=4] {'shard'}, dimensions={0} | all-to-all | bytes 1605632 | tf_op jit(solution)/shard_map/all_to_all | solution.py:462
  157.7 3.9 %all-to-all-start.5 = ((bf16[32,152,128]{2,1,0:T(8,128)(2,1)}), bf16[32,152,128]{2,1,0:T(8,128)(2,1)S(1)}, u32[]{:S(2)}, u32[]{:S(2)}) async-start(bf16[32,152,128]{2,1,0:T(8,128)(2,1)} %get-tuple-element.53), calls=%async_computation.5 | async-start | bytes 2490368 | tf_op jit(solution)/shard_map/all_to_all | solution.py:381
  161.7 1.3 copy-done.11
  162.9 1.3 copy-done.27
  164.2 2.2 value.1
  166.5 14.3 %all-to-all-done.5.pay = bf16[32,152,128]{2,1,0:T(8,128)(2,1)S(1)} async-done(((bf16[32,152,128]{2,1,0:T(8,128)(2,1)}), bf16[32,152,128]{2,1,0:T(8,128)(2,1)S(1)}, u32[]{:S(2)}, u32[]{:S(2)}) %all-to-all-start.5) | async-done | bytes 1245216 | tf_op jit(solution)/shard_map/all_to_all | solution.py:381
  181.9 4.7 %all-to-all-start.2 = ((bf16[128,40,128]{2,1,0:T(8,128)(2,1)}), bf16[128,40,128]{2,1,0:T(8,128)(2,1)S(1)}, u32[]{:S(2)}, u32[]{:S(2)}) async-start(bf16[128,40,128]{2,1,0:T(8,128)(2,1)} %bitcast.9), calls=%async_computation.2 | async-start | bytes 2621440 | tf_op jit(solution)/shard_map/all_to_all | solution.py:385
  186.5 1.3 copy-done.7
  187.8 1.3 sum_gradients.1
  189.1 19.2 %all-to-all-done.2 = bf16[128,40,128]{2,1,0:T(8,128)(2,1)S(1)} async-done(((bf16[128,40,128]{2,1,0:T(8,128)(2,1)}), bf16[128,40,128]{2,1,0:T(8,128)(2,1)S(1)}, u32[]{:S(2)}, u32[]{:S(2)}) %all-to-all-start.2) | async-done | bytes 1310752 | tf_op jit(solution)/shard_map/all_to_all | solution.py:385
  209.3 4.2 %all-to-all-start.6 = ((bf16[32,160,128]{2,1,0:T(8,128)(2,1)}), bf16[32,160,128]{2,1,0:T(8,128)(2,1)S(1)}, u32[]{:S(2)}, u32[]{:S(2)}) async-start(bf16[32,160,128]{2,1,0:T(8,128)(2,1)} %sum_gradients.1), calls=%async_computation.6 | async-start | bytes 2621440 | tf_op jit(solution)/shard_map/all_to_all | solution.py:381
  214.3 1.3 copy-done.5
  216.9 3.9 %convolution_bitcast_fusion = f32[1,768,768]{2,1,0:T(8,128)} fusion(bf16[768,768]{1,0:T(8,128)(2,1)} %copy-done.26, bf16[768,768]{1,0:T(8,128)(2,1)S(1)} %bitcast.29, f32[768]{0:T(1024)S(1)} %copy-done.50), kind=kOutput, calls=%fused_computation.1 | convolution fusion | flops 907739136 | bytes 4721664 | tf_op jit(solution)/shard_map/dot_general | solution.py:28
  220.8 2.4 collective-permute-start.7
  226.8 2.5 %collective-permute-start.14 = (bf16[128,768]{1,0:T(8,128)(2,1)S(1)}, bf16[128,768]{1,0:T(8,128)(2,1)S(1)}, u32[]{:S(2)}, u32[]{:S(2)}) collective-permute-start(bf16[128,768]{1,0:T(8,128)(2,1)S(1)} %token_grad.1.t0), channel_id=1, source_target_pairs={{0,3},{1,0},{2,1},{3,2},{4,7},{5,4},{6,5},{7,6},{8,11},{9,8},{10,9... | collective-permute-start | bytes 589832 | tf_op jit(solution)/shard_map/ppermute | solution.py:389
  229.4 2.5 %convolution_bitcast_fusion.1 = f32[1,768,768]{2,1,0:T(8,128)} fusion(bf16[768,768]{1,0:T(8,128)(2,1)S(1)} %bitcast.25, bf16[768,768]{1,0:T(8,128)(2,1)S(1)} %copy-done.47), kind=kOutput, calls=%fused_computation.2 | convolution fusion | flops 905969664 | bytes 4718592 | tf_op jit(solution)/shard_map/dot_general | solution.py:28
  231.9 2.3 collective-permute-done.8.p3
  234.3 1.3 result.1
  235.5 2.1 collective-permute-done.13.t2
  237.7 4.0 %collective-permute-done.14.t3 = bf16[128,768]{1,0:T(8,128)(2,1)S(1)} collective-permute-done((bf16[128,768]{1,0:T(8,128)(2,1)S(1)}, bf16[128,768]{1,0:T(8,128)(2,1)S(1)}, u32[]{:S(2)}, u32[]{:S(2)}) %collective-permute-start.14) | collective-permute-done | bytes 196640 | tf_op jit(solution)/shard_map/ppermute | solution.py:389
  243.8 1.4 copy-done.20
  245.2 2.9 %copy.34 = f32[3,768,192]{1,2,0:T(8,128)} copy(f32[3,768,192]{2,1,0:T(8,128)} %copy-done.20) | data formatting | bytes 3538944
  (128 shorter events, 34.4 us)
Async XLA Ops:
  4.3 8.4 %copy-start.23 = (bf16[192,768]{1,0:T(8,128)(2,1)S(1)}, bf16[192,768]{1,0:T(8,128)(2,1)}, u32[]{:S(2)}) copy-start(bf16[192,768]{1,0:T(8,128)(2,1)} %out_proj.1) | copy-start | bytes 884740
  4.3 42.0 %all-to-all-start.1 = ((bf16[32,24,768]{2,1,0:T(8,128)(2,1)}), bf16[32,24,768]{2,1,0:T(8,128)(2,1)S(1)}, u32[]{:S(2)}, u32[]{:S(2)}) async-start(bf16[32,24,768]{2,1,0:T(8,128)(2,1)} %dispatch_cotangent.1), calls=%async_computation.1 | async-start | bytes 2359296 | tf_op jit(solution)/shard_map/all_to_all | solution.py:381
  12.7 7.5 %copy-start.51 = (s32[1023]{0:T(1024)S(1)}, s32[1023]{0:T(1024)}, u32[]{:S(2)}) copy-start(s32[1023]{0:T(1024)} %param.22) | copy-start | bytes 12280
  12.7 7.7 %copy-start.2 = (bf16[512,768]{1,0:T(8,128)(2,1)S(1)}, bf16[512,768]{1,0:T(8,128)(2,1)}, u32[]{:S(2)}) copy-start(bf16[512,768]{1,0:T(8,128)(2,1)} %tok.5) | copy-start | bytes 2359300
  12.7 7.7 %copy-start.43 = (f32[2,768]{1,0:T(2,128)S(1)}, f32[2,768]{1,0:T(2,128)}, u32[]{:S(2)}) copy-start(f32[2,768]{1,0:T(2,128)} %gains.9) | copy-start | bytes 18436
  12.7 7.7 %copy-start.45 = (f32[3,32]{1,0:T(4,128)S(1)}, f32[3,32]{1,0:T(4,128)}, u32[]{:S(2)}) copy-start(f32[3,32]{1,0:T(4,128)} %rb.1) | copy-start | bytes 1156
  12.7 16.7 %collective-permute-start.3 = (bf16[192,768]{1,0:T(8,128)(2,1)S(1)}, bf16[192,768]{1,0:T(8,128)(2,1)}, u32[]{:S(2)}, u32[]{:S(2)}) collective-permute-start(bf16[192,768]{1,0:T(8,128)(2,1)S(1)} %copy-done.23), channel_id=1, source_target_pairs={{0,1},{1,2},{2,3},{3,0},{4,5},{5,6},{6,7},{7,4},{8,9},{9,10},{10,1... | collective-permute-start | bytes 884744 | tf_op jit(solution)/shard_map/ppermute | solution.py:389
  14.4 17.1 %collective-permute-start.4 = (bf16[192,768]{1,0:T(8,128)(2,1)S(1)}, bf16[192,768]{1,0:T(8,128)(2,1)}, u32[]{:S(2)}, u32[]{:S(2)}) collective-permute-start(bf16[192,768]{1,0:T(8,128)(2,1)S(1)} %copy-done.23), channel_id=1, source_target_pairs={{0,2},{1,3},{2,0},{3,1},{4,6},{5,7},{6,4},{7,5},{8,10},{9,11},{10,... | collective-permute-start | bytes 884744 | tf_op jit(solution)/shard_map/ppermute | solution.py:389
  17.3 14.2 %collective-permute-start.5 = (bf16[192,768]{1,0:T(8,128)(2,1)S(1)}, bf16[192,768]{1,0:T(8,128)(2,1)}, u32[]{:S(2)}, u32[]{:S(2)}) collective-permute-start(bf16[192,768]{1,0:T(8,128)(2,1)S(1)} %copy-done.23), channel_id=1, source_target_pairs={{0,3},{1,0},{2,1},{3,2},{4,7},{5,4},{6,5},{7,6},{8,11},{9,8},{10,9... | collective-permute-start | bytes 884744 | tf_op jit(solution)/shard_map/ppermute | solution.py:389
  20.1 12.7 %copy-start = (bf16[3,768,192]{2,1,0:T(8,128)(2,1)}, bf16[3,768,192]{2,1,0:T(8,128)(2,1)S(1)}, u32[]{:S(2)}) copy-start(bf16[3,768,192]{2,1,0:T(8,128)(2,1)S(1)} %copy.27.w) | copy-start | bytes 2654212
  27.9 12.0 %collective-permute-start = (bf16[768,128]{1,0:T(8,128)(2,1)}, bf16[768,128]{1,0:T(8,128)(2,1)}, u32[]{:S(2)}, u32[]{:S(2)}) collective-permute-start(bf16[768,128]{1,0:T(8,128)(2,1)} %get-tuple-element.35.h0), channel_id=1, source_target_pairs={{0,1},{1,2},{2,3},{3,0},{4,5},{5,6},{6,7},{7,4},{8,9},{9,10},{10,1... | collective-permute-start | bytes 589832 | tf_op jit(solution)/shard_map/ppermute | solution.py:389
  28.6 11.3 %collective-permute-start.1 = (bf16[768,128]{1,0:T(8,128)(2,1)}, bf16[768,128]{1,0:T(8,128)(2,1)}, u32[]{:S(2)}, u32[]{:S(2)}) collective-permute-start(bf16[768,128]{1,0:T(8,128)(2,1)} %get-tuple-element.35.h0), channel_id=1, source_target_pairs={{0,2},{1,3},{2,0},{3,1},{4,6},{5,7},{6,4},{7,5},{8,10},{9,11},{10,... | collective-permute-start | bytes 589832 | tf_op jit(solution)/shard_map/ppermute | solution.py:389
  29.4 11.1 %collective-permute-start.2 = (bf16[768,128]{1,0:T(8,128)(2,1)}, bf16[768,128]{1,0:T(8,128)(2,1)}, u32[]{:S(2)}, u32[]{:S(2)}) collective-permute-start(bf16[768,128]{1,0:T(8,128)(2,1)} %get-tuple-element.35.h0), channel_id=1, source_target_pairs={{0,3},{1,0},{2,1},{3,2},{4,7},{5,4},{6,5},{7,6},{8,11},{9,8},{10,9... | collective-permute-start | bytes 589832 | tf_op jit(solution)/shard_map/ppermute | solution.py:389
  47.4 7.4 %copy-start.48 = (bf16[768,32]{0,1:T(8,128)(2,1)S(1)}, bf16[768,32]{0,1:T(8,128)(2,1)}, u32[]{:S(2)}) copy-start(bf16[768,32]{0,1:T(8,128)(2,1)} %param.17) | copy-start | bytes 147460
  47.4 7.6 %copy-start.10 = (bf16[1,768,768]{2,1,0:T(8,128)(2,1)S(1)}, bf16[1,768,768]{2,1,0:T(8,128)(2,1)}, u32[]{:S(2)}) copy-start(bf16[1,768,768]{2,1,0:T(8,128)(2,1)} %param.19) | copy-start | bytes 3538948
  47.4 25.8 %all-to-all-start = ((bf16[32,24,768]{2,1,0:T(8,128)(2,1)}), bf16[32,24,768]{2,1,0:T(8,128)(2,1)S(1)}, u32[]{:S(2)}, u32[]{:S(2)}) async-start(bf16[32,24,768]{2,1,0:T(8,128)(2,1)} %copy-done.28), calls=%async_computation | async-start | bytes 2359296 | tf_op jit(solution)/shard_map/all_to_all | solution.py:381
  57.4 1.4 copy-start.1
  73.1 8.0 %copy-start.8 = (bf16[32,24,768]{2,1,0:T(8,128)(2,1)}, bf16[32,24,768]{2,1,0:T(8,128)(2,1)S(1)}, u32[]{:S(2)}) copy-start(bf16[32,24,768]{2,1,0:T(8,128)(2,1)S(1)} %all-to-all-done) | copy-start | bytes 3538948
  73.2 1.7 copy-start.25
  84.0 27.8 %all-to-all-start.3 = ((bf16[128,40,128]{2,1,0:T(8,128)(2,1)}), bf16[128,40,128]{2,1,0:T(8,128)(2,1)S(1)}, u32[]{:S(2)}, u32[]{:S(2)}) async-start(bf16[128,40,128]{2,1,0:T(8,128)(2,1)} %bitcast.36), calls=%async_computation.3 | async-start | bytes 2621440 | tf_op jit(solution)/shard_map/all_to_all | solution.py:385
  90.0 27.4 %copy-start.49 = (s32[512]{0:T(512)S(1)}, s32[512]{0:T(512)}, u32[]{:S(2)}) copy-start(s32[512]{0:T(512)} %param.20) | copy-start | bytes 6148
  111.8 15.4 %copy-start.16 = (bf16[512,768]{1,0:T(8,128)(2,1)S(1)}, bf16[512,768]{1,0:T(8,128)(2,1)}, u32[]{:S(2)}) copy-start(bf16[512,768]{1,0:T(8,128)(2,1)} %cot.1) | copy-start | bytes 2359300
  111.8 15.4 %copy-start.42 = (bf16[192,512]{1,0:T(8,128)(2,1)S(1)}, bf16[192,512]{1,0:T(8,128)(2,1)}, u32[]{:S(2)}) copy-start(bf16[192,512]{1,0:T(8,128)(2,1)} %copy-done.41) | copy-start | bytes 589828
  114.1 13.0 %copy-start.36 = (bf16[512,192]{1,0:T(8,128)(2,1)S(1)}, bf16[512,192]{1,0:T(8,128)(2,1)}, u32[]{:S(2)}) copy-start(bf16[512,192]{1,0:T(8,128)(2,1)} %copy-done.35) | copy-start | bytes 589828
  114.1 9.4 %collective-permute-start.10 = (bf16[768,128]{1,0:T(8,128)(2,1)}, bf16[768,128]{1,0:T(8,128)(2,1)S(1)}, u32[]{:S(2)}, u32[]{:S(2)}) collective-permute-start(bf16[768,128]{1,0:T(8,128)(2,1)} %get-tuple-element.42.p0), channel_id=1, source_target_pairs={{0,2},{1,3},{2,0},{3,1},{4,6},{5,7},{6,4},{7,5},{8,10},{9,11},{10,... | collective-permute-start | bytes 589832 | tf_op jit(solution)/shard_map/ppermute | solution.py:389
  115.0 10.1 %collective-permute-start.11 = (bf16[768,128]{1,0:T(8,128)(2,1)}, bf16[768,128]{1,0:T(8,128)(2,1)S(1)}, u32[]{:S(2)}, u32[]{:S(2)}) collective-permute-start(bf16[768,128]{1,0:T(8,128)(2,1)} %get-tuple-element.42.p0), channel_id=1, source_target_pairs={{0,3},{1,0},{2,1},{3,2},{4,7},{5,4},{6,5},{7,6},{8,11},{9,8},{10,9... | collective-permute-start | bytes 589832 | tf_op jit(solution)/shard_map/ppermute | solution.py:389
  117.5 9.7 %collective-permute-start.9 = (bf16[768,128]{1,0:T(8,128)(2,1)}, bf16[768,128]{1,0:T(8,128)(2,1)S(1)}, u32[]{:S(2)}, u32[]{:S(2)}) collective-permute-start(bf16[768,128]{1,0:T(8,128)(2,1)} %get-tuple-element.42.p0), channel_id=1, source_target_pairs={{0,1},{1,2},{2,3},{3,0},{4,5},{5,6},{6,7},{7,4},{8,9},{9,10},{10,1... | collective-permute-start | bytes 589832 | tf_op jit(solution)/shard_map/ppermute | solution.py:389
  118.8 8.4 %copy-start.40 = (f32[512,1]{1,0:T(8,128)S(1)}, f32[512,1]{1,0:T(8,128)}, u32[]{:S(2)}) copy-start(f32[512,1]{1,0:T(8,128)} %copy-done.39) | copy-start | bytes 6148
  157.7 23.1 %all-to-all-start.5 = ((bf16[32,152,128]{2,1,0:T(8,128)(2,1)}), bf16[32,152,128]{2,1,0:T(8,128)(2,1)S(1)}, u32[]{:S(2)}, u32[]{:S(2)}) async-start(bf16[32,152,128]{2,1,0:T(8,128)(2,1)} %get-tuple-element.53), calls=%async_computation.5 | async-start | bytes 2490368 | tf_op jit(solution)/shard_map/all_to_all | solution.py:381
  181.9 26.4 %all-to-all-start.2 = ((bf16[128,40,128]{2,1,0:T(8,128)(2,1)}), bf16[128,40,128]{2,1,0:T(8,128)(2,1)S(1)}, u32[]{:S(2)}, u32[]{:S(2)}) async-start(bf16[128,40,128]{2,1,0:T(8,128)(2,1)} %bitcast.9), calls=%async_computation.2 | async-start | bytes 2621440 | tf_op jit(solution)/shard_map/all_to_all | solution.py:385
  186.5 1.3 copy-start.7
  189.1 24.4 %copy-start.34 = (f32[768,1]{1,0:T(8,128)S(1)}, f32[768,1]{1,0:T(8,128)}, u32[]{:S(2)}) copy-start(f32[768,1]{1,0:T(8,128)} %copy-done.33) | copy-start | bytes 9220
  209.3 33.2 %all-to-all-start.6 = ((bf16[32,160,128]{2,1,0:T(8,128)(2,1)}), bf16[32,160,128]{2,1,0:T(8,128)(2,1)S(1)}, u32[]{:S(2)}, u32[]{:S(2)}) async-start(bf16[32,160,128]{2,1,0:T(8,128)(2,1)} %sum_gradients.1), calls=%async_computation.6 | async-start | bytes 2621440 | tf_op jit(solution)/shard_map/all_to_all | solution.py:381
  214.3 1.3 copy-start.5
  215.6 1.3 copy-start.50
  216.1 7.9 %copy-start.22 = (f32[512,768]{1,0:T(8,128)S(1)}, f32[512,768]{1,0:T(8,128)}, u32[]{:S(2)}) copy-start(f32[512,768]{1,0:T(8,128)} %get-tuple-element.52.dhid) | copy-start | bytes 4718596
  216.2 7.9 %copy-start.44 = (f32[2,768]{1,0:T(2,128)S(1)}, f32[2,768]{1,0:T(2,128)}, u32[]{:S(2)}) copy-start(f32[2,768]{1,0:T(2,128)} %gains.9) | copy-start | bytes 18436
  216.2 10.7 %collective-permute-start.6 = (bf16[768,128]{1,0:T(8,128)(2,1)S(1)}, bf16[768,128]{1,0:T(8,128)(2,1)S(1)}, u32[]{:S(2)}, u32[]{:S(2)}) collective-permute-start(bf16[768,128]{1,0:T(8,128)(2,1)S(1)} %collect_value.1.p0), channel_id=1, source_target_pairs={{0,1},{1,2},{2,3},{3,0},{4,5},{5,6},{6,7},{7,4},{8,9},{9,10},{10,1... | collective-permute-start | bytes 589832 | tf_op jit(solution)/shard_map/ppermute | solution.py:389
  220.8 11.2 %collective-permute-start.7 = (bf16[768,128]{1,0:T(8,128)(2,1)S(1)}, bf16[768,128]{1,0:T(8,128)(2,1)S(1)}, u32[]{:S(2)}, u32[]{:S(2)}) collective-permute-start(bf16[768,128]{1,0:T(8,128)(2,1)S(1)} %collect_value.1.p0), channel_id=1, source_target_pairs={{0,2},{1,3},{2,0},{3,1},{4,6},{5,7},{6,4},{7,5},{8,10},{9,11},{10,... | collective-permute-start | bytes 589832 | tf_op jit(solution)/shard_map/ppermute | solution.py:389
  223.1 11.1 %collective-permute-start.8 = (bf16[768,128]{1,0:T(8,128)(2,1)S(1)}, bf16[768,128]{1,0:T(8,128)(2,1)S(1)}, u32[]{:S(2)}, u32[]{:S(2)}) collective-permute-start(bf16[768,128]{1,0:T(8,128)(2,1)S(1)} %collect_value.1.p0), channel_id=1, source_target_pairs={{0,3},{1,0},{2,1},{3,2},{4,7},{5,4},{6,5},{7,6},{8,11},{9,8},{10,9... | collective-permute-start | bytes 589832 | tf_op jit(solution)/shard_map/ppermute | solution.py:389
  224.1 5.3 %copy-start.9 = (bf16[32,24,768]{2,1,0:T(8,128)(2,1)S(1)}, bf16[32,24,768]{2,1,0:T(8,128)(2,1)}, u32[]{:S(2)}) copy-start(bf16[32,24,768]{2,1,0:T(8,128)(2,1)} %copy-done.8) | copy-start | bytes 3538948
  224.1 5.3 %copy-start.47 = (bf16[768,768]{1,0:T(8,128)(2,1)S(1)}, bf16[768,768]{1,0:T(8,128)(2,1)}, u32[]{:S(2)}) copy-start(bf16[768,768]{1,0:T(8,128)(2,1)} %copy-done.46) | copy-start | bytes 3538948
  224.4 11.1 %collective-permute-start.12 = (bf16[128,768]{1,0:T(8,128)(2,1)S(1)}, bf16[128,768]{1,0:T(8,128)(2,1)S(1)}, u32[]{:S(2)}, u32[]{:S(2)}) collective-permute-start(bf16[128,768]{1,0:T(8,128)(2,1)S(1)} %token_grad.1.t0), channel_id=1, source_target_pairs={{0,1},{1,2},{2,3},{3,0},{4,5},{5,6},{6,7},{7,4},{8,9},{9,10},{10,1... | collective-permute-start | bytes 589832 | tf_op jit(solution)/shard_map/ppermute | solution.py:389
  225.6 12.0 %collective-permute-start.13 = (bf16[128,768]{1,0:T(8,128)(2,1)S(1)}, bf16[128,768]{1,0:T(8,128)(2,1)S(1)}, u32[]{:S(2)}, u32[]{:S(2)}) collective-permute-start(bf16[128,768]{1,0:T(8,128)(2,1)S(1)} %token_grad.1.t0), channel_id=1, source_target_pairs={{0,2},{1,3},{2,0},{3,1},{4,6},{5,7},{6,4},{7,5},{8,10},{9,11},{10,... | collective-permute-start | bytes 589832 | tf_op jit(solution)/shard_map/ppermute | solution.py:389
  226.8 14.8 %collective-permute-start.14 = (bf16[128,768]{1,0:T(8,128)(2,1)S(1)}, bf16[128,768]{1,0:T(8,128)(2,1)S(1)}, u32[]{:S(2)}, u32[]{:S(2)}) collective-permute-start(bf16[128,768]{1,0:T(8,128)(2,1)S(1)} %token_grad.1.t0), channel_id=1, source_target_pairs={{0,3},{1,0},{2,1},{3,2},{4,7},{5,4},{6,5},{7,6},{8,11},{9,8},{10,9... | collective-permute-start | bytes 589832 | tf_op jit(solution)/shard_map/ppermute | solution.py:389
  229.4 4.9 %copy-start.3 = (f32[512,768]{1,0:T(8,128)S(1)}, f32[512,768]{1,0:T(8,128)}, u32[]{:S(2)}) copy-start(f32[512,768]{1,0:T(8,128)} %get-tuple-element.40.hidden.hidden_in) | copy-start | bytes 4718596
  229.4 4.9 %copy-start.38 = (f32[512,1]{1,0:T(8,128)S(1)}, f32[512,1]{1,0:T(8,128)}, u32[]{:S(2)}) copy-start(f32[512,1]{1,0:T(8,128)} %copy-done.37) | copy-start | bytes 6148
  243.8 1.4 copy-start.20
  (25 other events, 25.0 us)
